TPU v7x, 32 devices: a whole 2x2x4 slice. The times are simulated.
32 devices in a mesh: seq: 4 (over x, core), vocab: 8 (over z, y).
Axes of the slice: x: 2, y: 2, z: 4, core: 2. Of those that a mesh axis runs over, the one named last changes fastest.
Arguments:
- hidden: bfloat16 [1024, 4096], P('seq'), may hold values from -48 to 48
- head_weight: bfloat16 [4096, 16384], P('seq', 'vocab'), may hold values from -0.09375 to 0.09375
- queries: float32 [8, 16384], P(None, 'vocab'), may hold values from 0 to 1, as said below
- passage_lengths: int32 [16], replicated, may hold values from 1 to 192, 1024 in all
- pairing: int32 [16], replicated, may hold values from 0 to 7
- doc_freq: int32 [16384], P('vocab'), may hold values from 0 to 4194304
Outputs:
- grad_hidden: bfloat16 [1024, 4096], P('seq', 'vocab')
- losses: float32 [2], replicated
Inputs may be any that keep to these rules, and one draw needn't show every extreme that they name: `queries`: entries are nonnegative.
All inputs are finite; a program needn't handle non-finite values.
Results may differ from a plain program's by a relative error of at most 0.0039.
Values may be sent and summed in bfloat16 or wider, within the bound.
A program may use at most 128 MiB of HBM per device.

v0:
```python
import jax
import jax.numpy as jnp
from jax import lax
from jax.sharding import PartitionSpec as P

DOCS = 4194304


sharpness = 8.0
loss_scale = 16384.0
flops_weight = 32.0
highest = lax.Precision.HIGHEST


def softmax_terms(scores, pair_rows):
    onehot = (jnp.arange(scores.shape[0], dtype=jnp.int32)[:, None] == pair_rows[None, :]).astype(
        jnp.float32
    )
    peak_score = jnp.max(scores, axis=0)
    shifted = jnp.exp(scores - peak_score[None, :])
    denominator = jnp.sum(shifted, axis=0)
    log_total = peak_score + jnp.log(denominator)
    losses_each = log_total - jnp.sum(onehot * scores, axis=0)
    return (losses_each, shifted / denominator[None, :] - onehot)


def per_device(hidden, head_weight, queries, passage_lengths, pairing, doc_freq):
    tok_rows = hidden.shape[0]
    vocab_cols = head_weight.shape[1]
    passages = passage_lengths.shape[0]
    vocab_total = vocab_cols * lax.axis_size("vocab")
    finish = jnp.cumsum(passage_lengths)
    starts = finish - passage_lengths
    position = lax.axis_index("seq") * tok_rows + jnp.arange(tok_rows, dtype=jnp.int32)
    member = (
        (position[None, :] >= starts[:, None]) & (position[None, :] < finish[:, None])
    ).astype(jnp.float32)
    counts = passage_lengths.astype(jnp.float32)
    weights_df = jnp.log(1.0 + DOCS / (1.0 + doc_freq.astype(jnp.float32)))
    flops_grad = loss_scale * flops_weight * 2.0 / (vocab_total * passages)
    full_head = lax.all_gather(head_weight, "seq", axis=0, tiled=True)
    logits = jnp.dot(hidden, full_head, preferred_element_type=jnp.float32)
    lifted = 1.0 + jax.nn.relu(logits)
    squared = lifted * lifted
    fourth = squared * squared
    powered = fourth * fourth
    local_sums = jnp.dot(member, powered, precision=highest)
    totals = lax.psum(local_sums, "seq")
    pooled = (jnp.log(totals) - jnp.log(counts)[:, None]) / sharpness
    col_mean = jnp.sum(pooled, axis=0) / passages
    flops_part = jnp.sum(weights_df * col_mean * col_mean) / vocab_total
    scores, flops_value = lax.psum(
        (jnp.dot(queries, pooled.T, precision=highest), flops_part), "vocab"
    )
    losses_each, probs = softmax_terms(scores, pairing)
    contrast = jnp.mean(losses_each)
    dscores = probs * (loss_scale / passages)
    dpooled = jnp.dot(dscores.T, queries, precision=highest) + flops_grad * weights_df * col_mean
    factor = dpooled / totals
    spread = lax.dot_general(member, factor, (((0,), (0,)), ((), ())), precision=highest)
    seventh = fourth * squared * lifted
    dlogits = jnp.where(logits > 0, spread * seventh, 0.0).astype(jnp.bfloat16)
    grad_cols = lax.psum_scatter(
        lax.dot_general(
            full_head, dlogits, (((1,), (1,)), ((), ())), preferred_element_type=jnp.float32
        ),
        "vocab",
        scatter_dimension=0,
        tiled=True,
    )
    losses = jnp.stack([contrast, flops_value])
    return (grad_cols.T.astype(jnp.bfloat16), losses)


def solution(mesh):
    placed = (P("seq", None), P("seq", "vocab"), P(None, "vocab"), P(), P(), P("vocab"))
    return jax.shard_map(
        per_device, mesh=mesh, in_specs=placed, out_specs=(P("seq", "vocab"), P()), check_vma=False
    )
```

profile of v0, /device:TPU:3, one launch (start us, length us, event | category | flops | bytes accessed | tf_op | source)
XLA Modules:
  0.0 293.7 jit_solution(1702173292230546630)
XLA Ops:
  7.2 0.0 copy-start
  7.2 0.0 copy-start.3
  7.2 0.0 all-gather.2.cloned.1.call-start
  7.2 0.7 all-gather.2.cloned.1.call-update
  7.9 0.0 all-reduce.3.cloned.1.call-start
  8.0 0.0 copy-done.3
  8.0 0.1 copy.9
  8.1 0.1 reduce
  8.2 107.8 %all-gather.2.cloned.1.call-done = bf16[4096,2048]{1,0:T(8,128)(2,1)} async-done(((bf16[1024,2048]{1,0:T(8,128)(2,1)}), bf16[4096,2048]{1,0:T(8,128)(2,1)}) %all-gather.2.cloned.1.call-update) | async-done | bytes 16777232 | tf_op jit(solution)/shard_map/all_gather | solution.py:41
  116.0 0.0 copy-done
  116.0 8.1 %fusion.31 = f32[256,2048]{1,0:T(8,128)S(1)} fusion(bf16[256,4096]{1,0:T(8,128)(2,1)S(1)} %copy-done, bf16[4096,2048]{1,0:T(8,128)(2,1)} %all-gather.2.cloned.1.call-done), kind=kOutput, calls=%fused_computation.51 | convolution fusion | flops 4294967296 | bytes 20971520 | tf_op jit(solution)/shard_map/dot_general | solution.py:42
  124.2 0.0 copy-start.5
  124.2 1.3 copy-done.5
  125.5 1.8 fusion.3
  127.3 0.0 all-reduce.3.cloned.1.call-update
  127.3 0.0 reduce-scatter.2.cloned.1.call-start
  127.4 30.5 %all-reduce.3.cloned.1.call-done = f32[16,2048]{1,0:T(8,128)} async-done(((f32[16,2048]{1,0:T(8,128)}), f32[16,2048]{1,0:T(8,128)}) %all-reduce.3.cloned.1.call-update) | async-done | bytes 131088 | tf_op jit(solution)/shard_map/psum | solution.py:48
  157.9 1.0 fusion.8
  158.9 0.0 copy-done.2
  158.9 0.6 fusion.11
  160.2 0.0 copy-done.1
  160.2 1.2 convolution_bitcast_fusion.1
  161.4 19.0 %all-reduce = (f32[8,16]{1,0:T(8,128)S(1)}, f32[1]{0:T(128)}) all-reduce(f32[8,16]{1,0:T(8,128)S(1)} %convolution_bitcast_fusion.1, f32[1]{0:T(128)} %bitcast.5), channel_id=1, replica_groups=mesh['seq'=4,'vocab'=8] {'vocab'}, use_global_device_ids=true, to_apply=%region_2.3 | all-reduce | flops 129 | bytes 1032 | tf_op jit(solution)/shard_map/psum | solution.py:52
  180.5 0.0 copy-done.4
  180.5 1.2 fusion.2
  181.7 3.2 %fusion.1 = bf16[256,2048]{1,0:T(8,128)(2,1)S(1)} fusion(f32[16,2048]{1,0:T(8,128)S(1)} %fusion.2, f32[256,2048]{1,0:T(8,128)} %copy-done.5, s32[256]{0:T(256)S(1)} %iota_add_fusion, s32[16]{0:T(128)S(1)} %reduce, s32[16]{0:T(128)S(1)} %sub.25), kind=kOutput, calls=%fused_computation.5 | convolution fusion | flops 105918464 | bytes 3277952 | tf_op jit(solution)/shard_map/dot_general | solution.py:60
  184.9 10.1 %convolution_bitcast_fusion = f32[4096,256]{0,1:T(8,128)} fusion(bf16[256,2048]{1,0:T(8,128)(2,1)S(1)} %fusion.1, bf16[4096,2048]{1,0:T(8,128)(2,1)} %all-gather.2.cloned.1.call-done), kind=kOutput, calls=%fused_computation | convolution fusion | flops 4294967296 | bytes 22020096 | tf_op jit(solution)/shard_map/dot_general | solution.py:64
  195.0 0.0 reduce-scatter.2.cloned.1.call-update
  195.0 0.6 subtract_reduce_fusion
  196.3 1.2 pad_maximum_fusion
  197.5 87.9 %reduce-scatter.2.cloned.1.call-done = f32[512,256]{0,1:T(8,128)} async-done(((f32[4096,256]{0,1:T(8,128)}), f32[512,256]{0,1:T(8,128)}) %reduce-scatter.2.cloned.1.call-update) | async-done | bytes 524304 | tf_op jit(solution)/shard_map/reduce_scatter | solution.py:63
  285.4 1.8 convert_bitcast_fusion
  (9 shorter events, 0.1 us)
Async XLA Ops:
  7.2 108.9 %copy-start = (bf16[256,4096]{1,0:T(8,128)(2,1)S(1)}, bf16[256,4096]{1,0:T(8,128)(2,1)}, u32[]{:S(2)}) copy-start(bf16[256,4096]{1,0:T(8,128)(2,1)} %param.6) | copy-start | bytes 6291460
  7.2 0.8 copy-start.3
  7.2 108.8 %all-gather.2.cloned.1.call-start = ((), (), s32[]{:S(2)}) async-start(), calls=%async_computation.1 | async-start | bytes 20971520 | tf_op jit(solution)/shard_map/all_gather | solution.py:41
  7.9 150.0 %all-reduce.3.cloned.1.call-start = ((), (), s32[]{:S(2)}) async-start(), calls=%async_computation.2 | async-start | bytes 262144 | tf_op jit(solution)/shard_map/psum | solution.py:48
  124.2 1.4 copy-start.5
  125.5 33.4 %copy-start.2 = (s32[2048]{0:T(1024)S(1)}, s32[2048]{0:T(1024)}, u32[]{:S(2)}) copy-start(s32[2048]{0:T(1024)} %param.11) | copy-start | bytes 24580
  125.5 34.7 %copy-start.1 = (f32[8,2048]{1,0:T(8,128)S(1)}, f32[8,2048]{1,0:T(8,128)}, u32[]{:S(2)}) copy-start(f32[8,2048]{1,0:T(8,128)} %param.8) | copy-start | bytes 196612
  125.5 55.0 %copy-start.4 = (s32[16]{0:T(128)S(1)}, s32[16]{0:T(128)}, u32[]{:S(2)}) copy-start(s32[16]{0:T(128)} %param.10) | copy-start | bytes 196
  127.3 158.1 %reduce-scatter.2.cloned.1.call-start = ((), (), s32[]{:S(2)}) async-start(), calls=%async_computation.3 | async-start | bytes 4718592 | tf_op jit(solution)/shard_map/reduce_scatter | solution.py:63
Sparse Core Ops, SparseCore 0:
  9.6 106.4 all-gather.1
  127.4 30.4 all-reduce.2
  195.1 90.1 reduce-scatter.1
where the time goes:
time: 295 us; the launch traced here: 294 us
  waiting for transfers between devices  227 us (77%)
  matrix products  25.5 us (9%)
  blocking collectives  19 us (6%)
  between operations  15.1 us (5%)
  other arithmetic  5.46 us (2%)
    all_gather x1, waiting for transfers between devices, per_device(): full_head = lax.all_gather(head_weight, 'seq', axis=0, tiled=True)  108 us
    reduce_scatter x1, waiting for transfers between devices, per_device(): lax.psum_scatter(lax.dot_general(full_head, dlogits, (((1,), (1,)), ((),...  87.9 us
    psum x1, waiting for transfers between devices, per_device(): totals = lax.psum(local_sums, 'seq')  30.5 us
    psum x1, blocking collectives, per_device(): lax.psum((jnp.dot(queries, pooled.T, precision=highest), flops_part), 'vo...  19 us
    dot_general x1, matrix products, per_device(): lax.dot_general(full_head, dlogits, (((1,), (1,)), ((), ())), preferred_e...  10.1 us
    dot_general x1, matrix products, per_device(): logits = jnp.dot(hidden, full_head, preferred_element_type=jnp.float32)  8.11 us
  transfers between devices with their start and end apart: 3, of which 3 were waited for; matrix products, arithmetic and copies ran while one was open for 1% of the time, Pallas kernels for 0%

commit v1 on v0

v1 whole, which is shorter than its diff:
```python
import functools

import jax
import jax.numpy as jnp
from jax import lax
from jax.experimental import pallas as pl
from jax.experimental.pallas import tpu as pltpu
from jax.sharding import PartitionSpec as P

DOCS = 4194304

sharpness = 8.0
loss_scale = 16384.0
flops_weight = 32.0
highest = lax.Precision.HIGHEST
MESH = pl.DeviceIdType.MESH
PART = jnp.int16
LEVELS = 32767.0
f32 = jnp.float32
bf16 = jnp.bfloat16
TILE = 256


def powers(logits):
    lifted = 1.0 + jnp.maximum(logits, 0.0)
    squared = lifted * lifted
    fourth = squared * squared
    return lifted, squared, fourth


def rows_at(start, size, unit=128):
    return pl.ds(pl.multiple_of(start, unit), size)


def kernel(
    n_seq, n_voc, n_sem,
    hid_in, head_in, queries, len_row, pair_row, freq,
    out, losses,
    hid, head,    hidf, headp, psend, precv, scale_out, scale_in, lg, tot, totals_ref, factor_ref, pay, pay_in, sc, dl,
    g_send, g_recv, g_keep, h_send, h_recv, acc, fin_send, fin_recv, ss, rs, ls,
):
    s, v = lax.axis_index("seq"), lax.axis_index("vocab")
    chips = n_seq // 2
    x, k = s // 2, s % 2
    mate = x * 2 + (1 - k)
    tok, width = hid_in.shape
    blk, voc = head_in.shape
    half = voc // 2
    dcols = 2 * blk
    passages = len_row.shape[1]
    n_q = queries.shape[0]
    ratio = n_voc // n_seq
    pairs = ratio // 2
    odd, quad = v % 2, v // 2
    n2 = n_voc // 2
    piece = width // n_voc
    chunk = tok // 2
    count = [0]
    sent = []

    def sems(n=1):
        first = count[0]
        count[0] += n
        assert count[0] <= n_sem
        return first

    def copy(src, dst, slot, to, recv=None):
        return pltpu.make_async_remote_copy(
            src_ref=src, dst_ref=dst, send_sem=ss.at[slot],
            recv_sem=rs.at[slot if recv is None else recv],
            device_id=to, device_id_type=MESH,
        )

    def go(*args):
        c = copy(*args)
        c.start()
        sent.append(c)

    t_s, t_v = quad // pairs, s * ratio + 2 * (quad % pairs) + odd
    f_s, f_v = v // ratio, 2 * (s * pairs + (v % ratio) // 2) + odd
    moved = jnp.logical_or(t_s != s, t_v != v)

    barrier = pltpu.get_barrier_semaphore()
    for r in range(1, n_seq):
        pl.semaphore_signal(barrier, inc=1, device_id=((s + r) % n_seq, v), device_id_type=MESH)
    for r in range(1, n_voc):
        pl.semaphore_signal(barrier, inc=1, device_id=(s, (v + r) % n_voc), device_id_type=MESH)

    load_head = pltpu.make_async_copy(head_in, head, ls.at[0])
    load_hid = pltpu.make_async_copy(hid_in, hid, ls.at[1])
    load_head.start()
    load_hid.start()

    @pl.when(moved)
    def _():
        pl.semaphore_signal(barrier, inc=1, device_id=(f_s, f_v), device_id_type=MESH)
        pl.semaphore_wait(barrier, n_seq - 1 + n_voc)

    @pl.when(jnp.logical_not(moved))
    def _():
        pl.semaphore_wait(barrier, n_seq - 1 + n_voc - 1)

    near = (s, v + 1 - 2 * odd)
    hid_slots = {}
    for off in range(1, chips):
        to = lax.rem(x + off, chips)
        hid_slots[off] = sems()
        go(
            hid_in.at[rows_at(odd * chunk, chunk), rows_at(to * dcols, dcols)],
            hidf.at[rows_at(s * tok + odd * chunk, chunk)],
            hid_slots[off], (to * 2 + k, v),
        )
    own_cols = rows_at(x * dcols, dcols)
    head_slot, mine_slot = sems(), sems()
    go(head_in.at[:, rows_at((1 - k) * half, half)], headp, head_slot, (mate, v))
    go(hid_in.at[:, own_cols], hidf.at[rows_at(s * tok, tok)], mine_slot, (mate, v))

    def arrived(dst, slot):
        copy(dst, dst, slot, (mate, v)).wait_recv()

    def multiply(src, row, n_rows, base, put):
        def body(t, carry):
            left = src[rows_at(row, n_rows), rows_at(base + k * blk, blk)]
            right = src[rows_at(row, n_rows), rows_at(base + (1 - k) * blk, blk)]
            own = head[:, rows_at(k * half + t * TILE, TILE)]
            other = headp[:, rows_at(t * TILE, TILE)]
            res = jnp.dot(left, own, preferred_element_type=f32)
            put(t, res + jnp.dot(right, other, preferred_element_type=f32))
            return carry

        lax.fori_loop(0, half // TILE, body, 0)

    def put_lg(row):
        def put(t, res):
            lg[rows_at(row, res.shape[0]), rows_at(t * TILE, TILE)] = res

        return put

    load_head.wait()
    load_hid.wait()
    arrived(headp, head_slot)
    multiply(hid, 0, tok, x * dcols, put_lg(k * tok))
    arrived(hidf.at[rows_at(mate * tok, tok)], mine_slot)
    multiply(hidf, mate * tok, tok, 0, put_lg((1 - k) * tok))

    p_slots, scale_slots = {}, {}
    diagonal = lax.broadcasted_iota(jnp.int32, (chunk, chunk), 0) == lax.broadcasted_iota(
        jnp.int32, (chunk, chunk), 1
    )
    near_slots = {}
    for c in range(2):
        rank = odd if c == 0 else 1 - odd
        for off in range(1, chips):
            frm = lax.rem(x + chips - off, chips)
            block = hidf.at[rows_at((frm * 2 + k) * tok + rank * chunk, chunk)]
            fwd = sems()
            if c == 0:
                arrived(block, hid_slots[off])
                near_slots[off] = sems()
                go(block, block, near_slots[off], near)
            else:
                arrived(block, near_slots[off])
            go(block, block, fwd, (mate, v))
            for which in range(2):
                core = k if which == 0 else 1 - k
                if which == 1:
                    arrived(hidf.at[rows_at((frm * 2 + core) * tok + rank * chunk, chunk)], fwd)
                at = core * tok + rank * chunk

                def put(t, res, off=off, at=at, index=core * 2 + rank):
                    top = jnp.maximum(jnp.max(jnp.abs(res), axis=1, keepdims=True), 1e-30)
                    whole = jnp.round(res * (LEVELS / top)).astype(jnp.int32)
                    psend[off - 1, rows_at(at, chunk), rows_at(t * TILE, TILE)] = whole.astype(PART)
                    step = jnp.sum(
                        jnp.where(diagonal, top * (1.0 / LEVELS), 0.0), axis=0, keepdims=True
                    )
                    scale_out[off - 1, index, pl.ds(t, 1), :] = step

                multiply(hidf, (frm * 2 + core) * tok + rank * chunk, chunk, 0, put)
                p_slots[off, c, which] = sems()
                part = pl.ds(pl.multiple_of(at, 128), chunk)
                go(
                    psend.at[off - 1, part], precv.at[off - 1, part],
                    p_slots[off, c, which], (frm * 2 + k, v),
                )
                scale_slots[off, c, which] = sems()
                go(
                    scale_out.at[off - 1, core * 2 + rank], scale_in.at[off - 1, core * 2 + rank],
                    scale_slots[off, c, which], (frm * 2 + k, v),
                )
    for c in range(2):
        rank = odd if c == 0 else 1 - odd
        for off in range(1, chips):
            for which in range(2):
                core = k if which == 0 else 1 - k
                part = rows_at(core * tok + rank * chunk, chunk)
                arrived(precv.at[off - 1, part], p_slots[off, c, which])
                arrived(scale_in.at[off - 1, core * 2 + rank], scale_slots[off, c, which])

    square = (passages, passages)
    upto_row = lax.broadcasted_iota(jnp.int32, square, 0)
    upto_col = lax.broadcasted_iota(jnp.int32, square, 1)

    def upright(row):
        shown = jnp.where(upto_row == upto_col, row.astype(f32), 0.0)
        return jnp.sum(shown, axis=1, keepdims=True)

    counts = upright(len_row[...])
    len_col = counts.astype(jnp.int32)
    pair_col = upright(pair_row[...]).astype(jnp.int32)
    finish_col = jnp.sum(
        jnp.where(upto_col <= upto_row, len_row[...].astype(f32), 0.0), axis=1, keepdims=True
    ).astype(jnp.int32)
    finish_row = jnp.sum(
        jnp.where(upto_row <= upto_col, counts, 0.0), axis=0, keepdims=True
    ).astype(jnp.int32)
    here = 2 * tok
    place = x * here
    pos_row = place + lax.broadcasted_iota(jnp.int32, (passages, here), 1)
    member = jnp.logical_and(pos_row >= finish_col - len_col, pos_row < finish_col).astype(f32)

    def sum_tile(t, carry):
        cols = rows_at(t * TILE, TILE)
        for off in range(1, chips):
            for index in range(4):
                part = slice(index * chunk, (index + 1) * chunk)
                step = jnp.sum(
                    jnp.where(diagonal, scale_in[off - 1, index, pl.ds(t, 1), :], 0.0),
                    axis=1, keepdims=True,
                )
                whole = precv[off - 1, part, cols].astype(jnp.int32)
                lg[part, cols] += whole.astype(f32) * step
        logits = lg[:, cols]
        fourth = powers(logits)[2]
        tot[x, :, cols] = jnp.dot(
            member, fourth * fourth, precision=highest, preferred_element_type=f32
        )
        return carry

    lax.fori_loop(0, half // TILE, sum_tile, 0)
    base = sems(chips)
    for off in range(1, chips):
        to = lax.rem(x + off, chips)
        go(tot.at[x], tot.at[x], base + off, (to * 2 + k, v))
    for off in range(1, chips):
        frm = lax.rem(x + chips - off, chips)
        arrived(tot.at[frm], base + off)
    totals = tot[0]
    for c in range(1, chips):
        totals = totals + tot[c]
    totals_ref[...] = totals
    pooled = (jnp.log(totals) - jnp.log(counts)) / sharpness
    col_mean = jnp.sum(pooled, axis=0, keepdims=True) / passages
    freqs = freq[:, rows_at(k * half, half)].astype(f32)
    weights_df = jnp.log(1.0 + DOCS / (1.0 + freqs))
    vocab_total = voc * n_voc
    q_half = queries[:, rows_at(k * half, half)]
    pay[...] = jnp.zeros_like(pay)
    for i in range(n_q):
        pay[0:passages, i : i + 1] = jnp.sum(pooled * q_half[i : i + 1, :], axis=1, keepdims=True)
    pay[passages : passages + 1, 0:1] = jnp.sum(
        weights_df * col_mean * col_mean, axis=1, keepdims=True
    )
    slot = sems()
    go(pay, pay_in, slot, (mate, v))
    arrived(pay_in, slot)
    sc[v] = pay[...] + pay_in[...]
    out_base, in_base = sems(n_voc), sems(n_voc)
    for r in range(1, n_voc):
        go(sc.at[v], sc.at[v], out_base + r, (s, lax.rem(v + r, n_voc)), in_base + v)
    for r in range(1, n_voc):
        frm = lax.rem(v + r, n_voc)
        arrived(sc.at[frm], in_base + frm)
    everything = sc[0]
    for c in range(1, n_voc):
        everything = everything + sc[c]
    scores = everything[0:passages, 0:n_q]
    flops_value = everything[passages : passages + 1, 0:1] / vocab_total
    onehot = (lax.broadcasted_iota(jnp.int32, (passages, n_q), 1) == pair_col).astype(f32)
    peak = jnp.max(scores, axis=1, keepdims=True)
    shifted = jnp.exp(scores - peak)
    denominator = jnp.sum(shifted, axis=1, keepdims=True)
    each = peak + jnp.log(denominator) - jnp.sum(onehot * scores, axis=1, keepdims=True)
    contrast = jnp.sum(each, axis=0, keepdims=True) / passages
    lane = lax.broadcasted_iota(jnp.int32, losses.shape, 1)
    losses[...] = jnp.where(lane == 0, contrast, flops_value)
    dscores = (shifted / denominator - onehot) * (loss_scale / passages)
    flops_grad = loss_scale * flops_weight * 2.0 / (vocab_total * passages)
    dpooled = flops_grad * weights_df * col_mean
    for i in range(n_q):
        dpooled = dpooled + dscores[:, i : i + 1] * q_half[i : i + 1, :]
    factor_ref[...] = dpooled / totals_ref[...]

    dl_slots, mate_slots, fwd_slots = {}, {}, {}
    starts_row = finish_row - len_row[...]
    for c in range(2):
        pos_col = place + c * tok + lax.broadcasted_iota(jnp.int32, (tok, passages), 0)
        belongs = jnp.logical_and(pos_col >= starts_row, pos_col < finish_row).astype(f32)

        def spread_tile(t, carry, c=c, belongs=belongs):
            cols = rows_at(t * TILE, TILE)
            logits = lg[c * tok : (c + 1) * tok, cols]
            lifted, squared, fourth = powers(logits)
            spread = jnp.dot(
                belongs, factor_ref[:, cols], precision=highest, preferred_element_type=f32
            )
            grad = jnp.where(logits > 0, spread * (fourth * squared * lifted), 0.0)
            dl[k, rows_at(place + c * tok, tok), cols] = grad.astype(bf16)
            return carry

        lax.fori_loop(0, half // TILE, spread_tile, 0)
        rows = dl.at[k, rows_at(place + c * tok, tok)]
        for off in range(1, chips):
            to = lax.rem(x + off, chips)
            dl_slots[off, c] = sems()
            go(rows, rows, dl_slots[off, c], (to * 2 + k, v))
        mate_slots[c] = sems()
        go(rows, rows, mate_slots[c], (mate, v))

    step = min(piece, TILE)

    def grad_piece(row, j, put):
        def body(t, carry):
            wide = rows_at(j * piece + t * step, step)
            res = None
            for h in range(2):
                one = lax.dot_general(
                    dl[h, rows_at(row, tok), :], head[wide, h * half : (h + 1) * half],
                    (((1,), (1,)), ((), ())), preferred_element_type=f32,
                )
                res = one if res is None else res + one
            put(rows_at(t * step, step), res)
            return carry

        lax.fori_loop(0, piece // step, body, 0)

    g_slots, h_slots = {}, {}
    h_in = sems(n2)

    def blocks(off):
        frm = lax.rem(x + chips - off, chips)
        return [(off * 2 + c, frm * 2 + c) for c in range(2)]

    def second_level(o, block):
        for jj in range(pairs):
            arrived(g_recv.at[o, jj], g_slots[o, jj])
            both = g_keep[o, jj] + g_recv[o, jj].astype(f32)
            q = block * pairs + jj
            h_slots[o, jj] = sems()

            @pl.when(q == quad)
            def _():
                acc[...] = both

            @pl.when(q != quad)
            def _():
                h_send[o, jj] = both.astype(bf16)
                copy(
                    h_send.at[o, jj], h_recv.at[quad], h_slots[o, jj],
                    (s, 2 * q + odd), h_in + quad,
                ).start()

    waiting = []
    for off in range(chips):
        frm = lax.rem(x + chips - off, chips)
        for c in range(2):
            o, block = off * 2 + c, frm * 2 + c
            if off > 0:
                while len(waiting) > (1 if o < n_seq - 1 else 0):
                    second_level(*waiting.pop(0))
                rows = dl.at[k, rows_at(block * tok, tok)]
                arrived(rows, dl_slots[off, c])
                fwd_slots[off, c] = sems()
                go(rows, rows, fwd_slots[off, c], (mate, v))
            rows = dl.at[1 - k, rows_at(block * tok, tok)]
            arrived(rows, mate_slots[c] if off == 0 else fwd_slots[off, c])
            for jj in range(pairs):

                def put_send(cols, res, o=o, jj=jj):
                    g_send[o, jj, :, cols] = res.astype(bf16)

                def put_keep(cols, res, o=o, jj=jj):
                    g_keep[o, jj, :, cols] = res

                grad_piece(block * tok, 2 * jj + 1 - odd, put_send)
                g_slots[o, jj] = sems()
                go(g_send.at[o, jj], g_recv.at[o, jj], g_slots[o, jj], near)
                grad_piece(block * tok, 2 * jj + odd, put_keep)
            waiting.append((o, block))
    for entry in waiting:
        second_level(*entry)

    total = acc[...]
    for r in range(1, n2):
        frm = lax.rem(quad + r, n2)
        arrived(h_recv.at[frm], h_in + frm)
        total = total + h_recv[frm].astype(f32)
    fin_send[...] = total.astype(bf16)
    last = sems()

    @pl.when(moved)
    def _():
        c = copy(fin_send, fin_recv, last, (t_s, t_v))
        c.start()
        c.wait_recv()
        out[...] = fin_recv[...]
        c.wait_send()

    @pl.when(jnp.logical_not(moved))
    def _():
        out[...] = fin_send[...]

    for off in range(chips):
        for o, block in blocks(off):
            for jj in range(pairs):
                q = block * pairs + jj

                @pl.when(q != quad)
                def _():
                    copy(
                        h_send.at[o, jj], h_recv.at[quad], h_slots[o, jj],
                        (s, 2 * q + odd), h_in + quad,
                    ).wait_send()

    for c in sent:
        c.wait_send()


def per_device(n_seq, n_voc, hidden, head_weight, queries, passage_lengths, pairing, doc_freq):
    tok, width = hidden.shape
    blk, voc = head_weight.shape
    passages, n_q = passage_lengths.shape[0], queries.shape[0]
    chips, half, n2 = n_seq // 2, voc // 2, n_voc // 2
    pairs = n_voc // n_seq // 2
    piece = width // n_voc
    others = max(chips - 1, 1)
    n_sem = 32 + 20 * chips + 3 * n_voc + n2 + 2 * n_seq * pairs
    pad = passages + 8
    vmem = pltpu.VMEM
    scratch = [
        vmem((tok, width), bf16),
        vmem((blk, voc), bf16),
        vmem((n_seq * tok, 2 * blk), bf16),
        vmem((blk, half), bf16),
        vmem((others, 2 * tok, half), PART),
        vmem((others, 2 * tok, half), PART),
        vmem((others, 4, half // TILE, tok // 2), f32),
        vmem((others, 4, half // TILE, tok // 2), f32),
        vmem((2 * tok, half), f32),
        vmem((chips, passages, half), f32),
        vmem((passages, half), f32),
        vmem((passages, half), f32),
        vmem((pad, 128), f32),
        vmem((pad, 128), f32),
        vmem((n_voc, pad, 128), f32),
        vmem((2, n_seq * tok, half), bf16),
        vmem((n_seq, pairs, tok, piece), bf16),
        vmem((n_seq, pairs, tok, piece), bf16),
        vmem((n_seq, pairs, tok, piece), f32),
        vmem((n_seq, pairs, tok, piece), bf16),
        vmem((n2, tok, piece), bf16),
        vmem((tok, piece), f32),
        vmem((tok, piece), bf16),
        vmem((tok, piece), bf16),
        pltpu.SemaphoreType.DMA((n_sem,)),
        pltpu.SemaphoreType.DMA((n_sem,)),
        pltpu.SemaphoreType.DMA((2,)),
    ]
    spec = pl.BlockSpec(memory_space=pltpu.VMEM)
    grad, losses = pl.pallas_call(
        functools.partial(kernel, n_seq, n_voc, n_sem),
        out_shape=(
            jax.ShapeDtypeStruct((tok, piece), bf16),
            jax.ShapeDtypeStruct((1, 128), f32),
        ),
        in_specs=[pl.BlockSpec(memory_space=pl.ANY)] * 2 + [spec] * 4,
        out_specs=(spec, spec),
        scratch_shapes=scratch,
        compiler_params=pltpu.CompilerParams(
            collective_id=0, has_side_effects=True, vmem_limit_bytes=56 * 1024 * 1024
        ),
    )(
        hidden, head_weight, queries, passage_lengths[None, :], pairing[None, :],
        doc_freq[None, :],
    )
    return grad, losses[0, :2]


def solution(mesh):
    placed = (P("seq", None), P("seq", "vocab"), P(None, "vocab"), P(), P(), P("vocab"))
    return jax.shard_map(
        functools.partial(per_device, mesh.shape["seq"], mesh.shape["vocab"]),
        mesh=mesh, in_specs=placed, out_specs=(P("seq", "vocab"), P()), check_vma=False,
    )
```

time: 295 us -> 125 us (0.42)
  waiting for transfers between devices: 227 us -> 0 us
  Pallas kernels: 0 us -> 121 us
  matrix products: 25.5 us -> 0 us
  blocking collectives: 19 us -> 0 us
  between operations: 15.1 us -> 0.64 us
  other arithmetic: 5.46 us -> 0 us
    pallas_call x0 -> x1, Pallas kernels: none -> 121 us  [per_device(): pl.pallas_call(functools.partial(kernel, n_seq, n_voc, n_sem), out_shape=...]
    all_gather x1 -> x0, waiting for transfers between devices: 108 us -> none  [per_device(): full_head = lax.all_gather(head_weight, 'seq', axis=0, tiled=True)]
    reduce_scatter x1 -> x0, waiting for transfers between devices: 87.9 us -> none  [per_device(): lax.psum_scatter(lax.dot_general(full_head, dlogits, (((1,), (1,)), ((),...]
    psum x1 -> x0, waiting for transfers between devices: 30.5 us -> none  [per_device(): totals = lax.psum(local_sums, 'seq')]
    dot_general x6 -> x0, matrix products: 25.5 us -> none  [the longest x1 10.1 us: per_device(): lax.dot_general(full_head, dlogits, (((1,), (1,)), ((), ())), preferred_e...]
    psum x1 -> x0, blocking collectives: 19 us -> none  [per_device(): lax.psum((jnp.dot(queries, pooled.T, precision=highest), flops_part), 'vo...]
  transfers between devices with their start and end apart: 3 -> 0, of which waited for: 3 -> 0; matrix products, arithmetic and copies ran while one was open for 1% -> 0% of each run, Pallas kernels for 0% -> 0%
where the time goes in v1:
time: 125 us; the launch traced here: 124 us
  Pallas kernels  121 us (97%)
  local copies, waits for them, and re-layouts  2.8 us (2%)
    pallas_call x1, Pallas kernels, per_device(): pl.pallas_call(functools.partial(kernel, n_seq, n_voc, n_sem), out_shape=...  121 us

profile of v1, /device:TPU:3, one launch (start us, length us, event | category | flops | bytes accessed | tf_op | source)
XLA Modules:
  0.0 124.5 jit_solution(10508863272445161450)
XLA Ops:
  0.6 121.0 %shard_map.77 = (bf16[256,512]{1,0:T(8,128)(2,1)}, f32[1,128]{1,0:T(1,128)}) custom-call(bf16[256,4096]{1,0:T(8,128)(2,1)} %hid_in.1, bf16[1024,2048]{1,0:T(8,128)(2,1)} %head_in.1, f32[8,2048]{1,0:T(8,128)} %queries.1, s32[1,16]{1,0:T(1,128)} %bitcast.6, s32[1,16]{1,0:T(1,128)} %bitcast.7, s32[1,2048]{1,0:T(1,128)} %bitcast.5), custom_call_target="tpu_custom_call" | custom-call | tf_op jit(solution)/shard_map/pallas_call | solution.py:470
  121.7 1.1 slice_bitcast_fusion
  122.8 1.7 %copy.9 = bf16[256,512]{1,0:T(8,128)(2,1)} copy(bf16[256,512]{1,0:T(8,128)(2,1)} %get-tuple-element.8) | data formatting | bytes 524288

commit v2 on v1

--- a/solution.py
+++ b/solution.py
@@ -37,7 +37,7 @@
     hid_in, head_in, queries, len_row, pair_row, freq,
     out, losses,
     hid, head,    hidf, headp, psend, precv, scale_out, scale_in, lg, tot, totals_ref, factor_ref, pay, pay_in, sc, dl,
-    g_send, g_recv, g_keep, h_send, h_recv, acc, fin_send, fin_recv, ss, rs, ls,
+    g_send, g_recv, g_keep, h_send, h_recv, fin_send, fin_recv, ss, rs, ls,
 ):
     s, v = lax.axis_index("seq"), lax.axis_index("vocab")
     chips = n_seq // 2
@@ -76,9 +76,15 @@
         c.start()
         sent.append(c)
 
-    t_s, t_v = quad // pairs, s * ratio + 2 * (quad % pairs) + odd
-    f_s, f_v = v // ratio, 2 * (s * pairs + (v % ratio) // 2) + odd
-    moved = jnp.logical_or(t_s != s, t_v != v)
+    share = tok // n2
+    home = v // ratio
+    diagonal_one = home == s
+
+    def target(block, jj):
+        return block, s * ratio + 2 * jj + odd
+
+    def source(r):
+        return home, 2 * r + odd
 
     barrier = pltpu.get_barrier_semaphore()
     for r in range(1, n_seq):
@@ -91,14 +97,21 @@
     load_head.start()
     load_hid.start()
 
-    @pl.when(moved)
+    for r in range(n2):
+
+        @pl.when(jnp.logical_not(jnp.logical_and(diagonal_one, quad == r)))
+        def _():
+            pl.semaphore_signal(barrier, inc=1, device_id=source(r), device_id_type=MESH)
+
+    peers = n_seq - 1 + n_voc - 1 + n2
+
+    @pl.when(diagonal_one)
     def _():
-        pl.semaphore_signal(barrier, inc=1, device_id=(f_s, f_v), device_id_type=MESH)
-        pl.semaphore_wait(barrier, n_seq - 1 + n_voc)
-
-    @pl.when(jnp.logical_not(moved))
+        pl.semaphore_wait(barrier, peers - 1)
+
+    @pl.when(jnp.logical_not(diagonal_one))
     def _():
-        pl.semaphore_wait(barrier, n_seq - 1 + n_voc - 1)
+        pl.semaphore_wait(barrier, peers)
 
     near = (s, v + 1 - 2 * odd)
     hid_slots = {}
@@ -334,40 +347,66 @@
 
         lax.fori_loop(0, piece // step, body, 0)
 
-    g_slots, h_slots = {}, {}
-    h_in = sems(n2)
-
-    def blocks(off):
-        frm = lax.rem(x + chips - off, chips)
-        return [(off * 2 + c, frm * 2 + c) for c in range(2)]
+    g_slots, h_slots, fin_slots = {}, {}, {}
+    fin_in = sems(n2)
+    mine = rows_at(quad * share, share, share)
 
     def second_level(o, block):
         for jj in range(pairs):
             arrived(g_recv.at[o, jj], g_slots[o, jj])
             both = g_keep[o, jj] + g_recv[o, jj].astype(f32)
-            q = block * pairs + jj
-            h_slots[o, jj] = sems()
-
-            @pl.when(q == quad)
+            g_keep[o, jj] = both
+            h_send[o, jj] = both.astype(bf16)
+            h_slots[o, jj] = sems(n2)
+            first = sems(n2)
+            for r in range(1, n2):
+                to = lax.rem(quad + r, n2)
+                go(
+                    h_send.at[o, jj, rows_at(to * share, share, share)], h_recv.at[o, jj, quad],
+                    first + r, (s, 2 * to + odd), h_slots[o, jj] + quad,
+                )
+
+    def third_level(o, block):
+        for jj in range(pairs):
+            total = g_keep[o, jj, mine, :]
+            for r in range(1, n2):
+                frm = lax.rem(quad + r, n2)
+                arrived(h_recv.at[o, jj, frm], h_slots[o, jj] + frm)
+                total = total + h_recv[o, jj, frm].astype(f32)
+            fin_send[o, jj] = total.astype(bf16)
+            fin_slots[o, jj] = sems()
+            t_s, t_v = target(block, jj)
+            stays = jnp.logical_and(t_s == s, t_v == v)
+
+            @pl.when(stays)
             def _():
-                acc[...] = both
-
-            @pl.when(q != quad)
+                fin_recv[mine, :] = fin_send[o, jj]
+
+            @pl.when(jnp.logical_not(stays))
             def _():
-                h_send[o, jj] = both.astype(bf16)
-                copy(
-                    h_send.at[o, jj], h_recv.at[quad], h_slots[o, jj],
-                    (s, 2 * q + odd), h_in + quad,
-                ).start()
-
-    waiting = []
+                deliver(o, jj, block).start()
+
+    def deliver(o, jj, block):
+        return copy(
+            fin_send.at[o, jj], fin_recv.at[mine], fin_slots[o, jj],
+            target(block, jj), fin_in + quad,
+        )
+
+    placed = []
     for off in range(chips):
         frm = lax.rem(x + chips - off, chips)
         for c in range(2):
             o, block = off * 2 + c, frm * 2 + c
-            if off > 0:
-                while len(waiting) > (1 if o < n_seq - 1 else 0):
-                    second_level(*waiting.pop(0))
+            placed.append((o, block))
+            if o >= 2:
+                if o == 2:
+                    second_level(*placed[0])
+                else:
+                    second_level(*placed[o - 2])
+                    third_level(*placed[o - 3])
+                    if o == n_seq - 1:
+                        second_level(*placed[o - 1])
+                        third_level(*placed[o - 2])
                 rows = dl.at[k, rows_at(block * tok, tok)]
                 arrived(rows, dl_slots[off, c])
                 fwd_slots[off, c] = sems()
@@ -386,41 +425,24 @@
                 g_slots[o, jj] = sems()
                 go(g_send.at[o, jj], g_recv.at[o, jj], g_slots[o, jj], near)
                 grad_piece(block * tok, 2 * jj + odd, put_keep)
-            waiting.append((o, block))
-    for entry in waiting:
-        second_level(*entry)
-
-    total = acc[...]
-    for r in range(1, n2):
-        frm = lax.rem(quad + r, n2)
-        arrived(h_recv.at[frm], h_in + frm)
-        total = total + h_recv[frm].astype(f32)
-    fin_send[...] = total.astype(bf16)
-    last = sems()
-
-    @pl.when(moved)
-    def _():
-        c = copy(fin_send, fin_recv, last, (t_s, t_v))
-        c.start()
-        c.wait_recv()
-        out[...] = fin_recv[...]
-        c.wait_send()
-
-    @pl.when(jnp.logical_not(moved))
-    def _():
-        out[...] = fin_send[...]
-
-    for off in range(chips):
-        for o, block in blocks(off):
-            for jj in range(pairs):
-                q = block * pairs + jj
-
-                @pl.when(q != quad)
-                def _():
-                    copy(
-                        h_send.at[o, jj], h_recv.at[quad], h_slots[o, jj],
-                        (s, 2 * q + odd), h_in + quad,
-                    ).wait_send()
+    third_level(*placed[n_seq - 2])
+    second_level(*placed[n_seq - 1])
+    third_level(*placed[n_seq - 1])
+
+    for r in range(n2):
+
+        @pl.when(jnp.logical_not(jnp.logical_and(diagonal_one, quad == r)))
+        def _():
+            arrived(fin_recv.at[pl.ds(r * share, share)], fin_in + r)
+
+    out[...] = fin_recv[...]
+    for o, block in placed:
+        for jj in range(pairs):
+            t_s, t_v = target(block, jj)
+
+            @pl.when(jnp.logical_not(jnp.logical_and(t_s == s, t_v == v)))
+            def _():
+                deliver(o, jj, block).wait_send()
 
     for c in sent:
         c.wait_send()
@@ -434,7 +456,7 @@
     pairs = n_voc // n_seq // 2
     piece = width // n_voc
     others = max(chips - 1, 1)
-    n_sem = 32 + 20 * chips + 3 * n_voc + n2 + 2 * n_seq * pairs
+    n_sem = 32 + 20 * chips + 3 * n_voc + n2 + n_seq * pairs * (2 * n2 + 2)
     pad = passages + 8
     vmem = pltpu.VMEM
     scratch = [
@@ -458,9 +480,8 @@
         vmem((n_seq, pairs, tok, piece), bf16),
         vmem((n_seq, pairs, tok, piece), f32),
         vmem((n_seq, pairs, tok, piece), bf16),
-        vmem((n2, tok, piece), bf16),
-        vmem((tok, piece), f32),
-        vmem((tok, piece), bf16),
+        vmem((n_seq, pairs, n2, tok // n2, piece), bf16),
+        vmem((n_seq, pairs, tok // n2, piece), bf16),
         vmem((tok, piece), bf16),
         pltpu.SemaphoreType.DMA((n_sem,)),
         pltpu.SemaphoreType.DMA((n_sem,)),

time: 125 us -> 113 us (0.904)
  Pallas kernels: 121 us -> 108 us
    pallas_call x1, Pallas kernels: 121 us -> 108 us  [per_device(): pl.pallas_call(functools.partial(kernel, n_seq, n_voc, n_sem), out_shape=...]
where the time goes in v2:
time: 113 us; the launch traced here: 112 us
  Pallas kernels  108 us (96%)
  local copies, waits for them, and re-layouts  2.8 us (2%)
    pallas_call x1, Pallas kernels, per_device(): pl.pallas_call(functools.partial(kernel, n_seq, n_voc, n_sem), out_shape=...  108 us

profile of v2, /device:TPU:3, one launch (start us, length us, event | category | flops | bytes accessed | tf_op | source)
XLA Modules:
  0.0 111.9 jit_solution(15421803146939713751)
XLA Ops:
  0.6 108.4 %shard_map.77 = (bf16[256,512]{1,0:T(8,128)(2,1)}, f32[1,128]{1,0:T(1,128)}) custom-call(bf16[256,4096]{1,0:T(8,128)(2,1)} %hid_in.1, bf16[1024,2048]{1,0:T(8,128)(2,1)} %head_in.1, f32[8,2048]{1,0:T(8,128)} %queries.1, s32[1,16]{1,0:T(1,128)} %bitcast.6, s32[1,16]{1,0:T(1,128)} %bitcast.7, s32[1,2048]{1,0:T(1,128)} %bitcast.5), custom_call_target="tpu_custom_call" | custom-call | tf_op jit(solution)/shard_map/pallas_call | solution.py:491
  109.1 1.1 %slice_bitcast_fusion = f32[2]{0:T(128)} fusion(f32[1,128]{1,0:T(1,128)} %get-tuple-element.5), kind=kLoop, calls=%fused_computation | loop fusion | bytes 16 | tf_op jit(solution)/shard_map/squeeze | solution.py:507
  110.2 1.7 %copy.9 = bf16[256,512]{1,0:T(8,128)(2,1)} copy(bf16[256,512]{1,0:T(8,128)(2,1)} %get-tuple-element.8) | data formatting | bytes 524288

commit v3 on v2

--- a/solution.py
+++ b/solution.py
@@ -323,22 +323,24 @@
 
         lax.fori_loop(0, half // TILE, spread_tile, 0)
         rows = dl.at[k, rows_at(place + c * tok, tok)]
-        for off in range(1, chips):
-            to = lax.rem(x + off, chips)
-            dl_slots[off, c] = sems()
-            go(rows, rows, dl_slots[off, c], (to * 2 + k, v))
+        for first in range(0, tok, chunk):
+            some = dl.at[k, rows_at(place + c * tok + first, chunk)]
+            for off in range(1, chips):
+                to = lax.rem(x + off, chips)
+                dl_slots[off, c, first] = sems()
+                go(some, some, dl_slots[off, c, first], (to * 2 + k, v))
         mate_slots[c] = sems()
         go(rows, rows, mate_slots[c], (mate, v))
 
     step = min(piece, TILE)
 
-    def grad_piece(row, j, put):
+    def grad_piece(row, n_rows, j, put):
         def body(t, carry):
             wide = rows_at(j * piece + t * step, step)
             res = None
             for h in range(2):
                 one = lax.dot_general(
-                    dl[h, rows_at(row, tok), :], head[wide, h * half : (h + 1) * half],
+                    dl[h, rows_at(row, n_rows), :], head[wide, h * half : (h + 1) * half],
                     (((1,), (1,)), ((), ())), preferred_element_type=f32,
                 )
                 res = one if res is None else res + one
@@ -353,7 +355,8 @@
 
     def second_level(o, block):
         for jj in range(pairs):
-            arrived(g_recv.at[o, jj], g_slots[o, jj])
+            for first, n_rows, slot in g_slots[o, jj]:
+                arrived(g_recv.at[o, jj, pl.ds(first, n_rows)], slot)
             both = g_keep[o, jj] + g_recv[o, jj].astype(f32)
             g_keep[o, jj] = both
             h_send[o, jj] = both.astype(bf16)
@@ -407,24 +410,32 @@
                     if o == n_seq - 1:
                         second_level(*placed[o - 1])
                         third_level(*placed[o - 2])
-                rows = dl.at[k, rows_at(block * tok, tok)]
-                arrived(rows, dl_slots[off, c])
-                fwd_slots[off, c] = sems()
-                go(rows, rows, fwd_slots[off, c], (mate, v))
-            rows = dl.at[1 - k, rows_at(block * tok, tok)]
-            arrived(rows, mate_slots[c] if off == 0 else fwd_slots[off, c])
-            for jj in range(pairs):
-
-                def put_send(cols, res, o=o, jj=jj):
-                    g_send[o, jj, :, cols] = res.astype(bf16)
-
-                def put_keep(cols, res, o=o, jj=jj):
-                    g_keep[o, jj, :, cols] = res
-
-                grad_piece(block * tok, 2 * jj + 1 - odd, put_send)
-                g_slots[o, jj] = sems()
-                go(g_send.at[o, jj], g_recv.at[o, jj], g_slots[o, jj], near)
-                grad_piece(block * tok, 2 * jj + odd, put_keep)
+            n_rows = tok if off == 0 else chunk
+            for first in range(0, tok, n_rows):
+                row = block * tok + first
+                if off > 0:
+                    some = dl.at[k, rows_at(row, n_rows)]
+                    arrived(some, dl_slots[off, c, first])
+                    fwd_slots[off, c, first] = sems()
+                    go(some, some, fwd_slots[off, c, first], (mate, v))
+                arrived(
+                    dl.at[1 - k, rows_at(row, n_rows)],
+                    mate_slots[c] if off == 0 else fwd_slots[off, c, first],
+                )
+                for jj in range(pairs):
+
+                    def put_send(cols, res, o=o, jj=jj, first=first, n_rows=n_rows):
+                        g_send[o, jj, first : first + n_rows, cols] = res.astype(bf16)
+
+                    def put_keep(cols, res, o=o, jj=jj, first=first, n_rows=n_rows):
+                        g_keep[o, jj, first : first + n_rows, cols] = res
+
+                    part = pl.ds(first, n_rows)
+                    grad_piece(row, n_rows, 2 * jj + 1 - odd, put_send)
+                    slot = sems()
+                    g_slots.setdefault((o, jj), []).append((first, n_rows, slot))
+                    go(g_send.at[o, jj, part], g_recv.at[o, jj, part], slot, near)
+                    grad_piece(row, n_rows, 2 * jj + odd, put_keep)
     third_level(*placed[n_seq - 2])
     second_level(*placed[n_seq - 1])
     third_level(*placed[n_seq - 1])
@@ -456,7 +467,7 @@
     pairs = n_voc // n_seq // 2
     piece = width // n_voc
     others = max(chips - 1, 1)
-    n_sem = 32 + 20 * chips + 3 * n_voc + n2 + n_seq * pairs * (2 * n2 + 2)
+    n_sem = 32 + 28 * chips + 2 * n_seq * pairs + 3 * n_voc + n2 + n_seq * pairs * (2 * n2 + 2)
     pad = passages + 8
     vmem = pltpu.VMEM
     scratch = [

time: 113 us -> 114 us (level)
  Pallas kernels: 108 us -> 110 us
    pallas_call x1, Pallas kernels: 108 us -> 110 us  [per_device(): pl.pallas_call(functools.partial(kernel, n_seq, n_voc, n_sem), out_shape=...]
where the time goes in v3:
time: 114 us
  Pallas kernels  110 us (96%)
  local copies, waits for them, and re-layouts  2.8 us (2%)
    pallas_call x1, Pallas kernels, per_device(): pl.pallas_call(functools.partial(kernel, n_seq, n_voc, n_sem), out_shape=...  110 us

profile of v3, /device:TPU:3, one launch (start us, length us, event | category | flops | bytes accessed | tf_op | source)
XLA Modules:
  0.0 113.7 jit_solution(10237141665665417196)
XLA Ops:
  0.6 110.3 %shard_map.77 = (bf16[256,512]{1,0:T(8,128)(2,1)}, f32[1,128]{1,0:T(1,128)}) custom-call(bf16[256,4096]{1,0:T(8,128)(2,1)} %hid_in.1, bf16[1024,2048]{1,0:T(8,128)(2,1)} %head_in.1, f32[8,2048]{1,0:T(8,128)} %queries.1, s32[1,16]{1,0:T(1,128)} %bitcast.6, s32[1,16]{1,0:T(1,128)} %bitcast.7, s32[1,2048]{1,0:T(1,128)} %bitcast.5), custom_call_target="tpu_custom_call" | custom-call | tf_op jit(solution)/shard_map/pallas_call | solution.py:502
  110.9 1.1 slice_bitcast_fusion
  112.1 1.7 %copy.9 = bf16[256,512]{1,0:T(8,128)(2,1)} copy(bf16[256,512]{1,0:T(8,128)(2,1)} %get-tuple-element.8) | data formatting | bytes 524288

commit v4 on v2

--- a/solution.py
+++ b/solution.py
@@ -330,7 +330,7 @@
         mate_slots[c] = sems()
         go(rows, rows, mate_slots[c], (mate, v))
 
-    step = min(piece, TILE)
+    step = min(piece, 2 * TILE)
 
     def grad_piece(row, j, put):
         def body(t, carry):

time: 113 us -> 112 us (level)
  no operation moved by 1% of the time
where the time goes in v4:
time: 112 us
  Pallas kernels  108 us (96%)
  local copies, waits for them, and re-layouts  2.8 us (2%)
    pallas_call x1, Pallas kernels, per_device(): pl.pallas_call(functools.partial(kernel, n_seq, n_voc, n_sem), out_shape=...  108 us

profile of v4, /device:TPU:3, one launch (start us, length us, event | category | flops | bytes accessed | tf_op | source)
XLA Modules:
  0.0 111.6 jit_solution(16375584153168742163)
XLA Ops:
  0.6 108.1 %shard_map.77 = (bf16[256,512]{1,0:T(8,128)(2,1)}, f32[1,128]{1,0:T(1,128)}) custom-call(bf16[256,4096]{1,0:T(8,128)(2,1)} %hid_in.1, bf16[1024,2048]{1,0:T(8,128)(2,1)} %head_in.1, f32[8,2048]{1,0:T(8,128)} %queries.1, s32[1,16]{1,0:T(1,128)} %bitcast.6, s32[1,16]{1,0:T(1,128)} %bitcast.7, s32[1,2048]{1,0:T(1,128)} %bitcast.5), custom_call_target="tpu_custom_call" | custom-call | tf_op jit(solution)/shard_map/pallas_call | solution.py:491
  108.8 1.1 %slice_bitcast_fusion = f32[2]{0:T(128)} fusion(f32[1,128]{1,0:T(1,128)} %get-tuple-element.5), kind=kLoop, calls=%fused_computation | loop fusion | bytes 16 | tf_op jit(solution)/shard_map/squeeze | solution.py:507
  109.9 1.7 %copy.9 = bf16[256,512]{1,0:T(8,128)(2,1)} copy(bf16[256,512]{1,0:T(8,128)(2,1)} %get-tuple-element.8) | data formatting | bytes 524288
